TPU v7x, 512 devices: a whole 4x8x8 slice. The times are simulated.
512 devices in a mesh: row: 16 (over x, z_hi), col: 32 (over z_lo, y, core).
Axes of the slice: x: 4, y: 8, z: 8 (z_hi: 4, z_lo: 2; z = z_hi * 2 + z_lo), core: 2. Of those that a mesh axis runs over, the one named last changes fastest.
Arguments:
- activations: bfloat16 [16384, 768], P('row', 'col'), may hold values from -6 to 6
- partner: int32 [64], replicated, may hold values from 0 to 63, each once
- mix_weight: int32 [64], replicated, may hold values from 0 to 256
- weight: bfloat16 [768, 24576], P(None, 'col'), may hold values from -0.15625 to 0.15625
- bias: float32 [24576], P('col'), may hold values from -3 to 3
- earlier: bfloat16 [16384, 24576], P('row', 'col'), may hold values from -5 to 5
- cotangent: bfloat16 [16384, 24576], P('row', 'col'), may hold values from -6 to 6
Outputs:
- hidden: bfloat16 [16384, 24576], P('row', 'col')
- weight_grad: float32 [768, 24576], P('row', 'col')
Inputs may be any that keep to these rules, and one draw needn't show every extreme that they name: `partner`: each image is named exactly once.
All inputs are finite; a program needn't handle non-finite values.
Results may differ from a plain program's by a relative error of at most 0.015.
Values may be sent and summed in bfloat16 or wider, within the bound.
A program may use at most 64 MiB of HBM per device.

v0:
```python
import jax
import jax.numpy as jnp
from jax import lax
from jax.sharding import PartitionSpec as P

PATCHES = 256
IMG_DEV = 4


def slope(preact):
    normal_cdf = 0.5 * (1.0 + lax.erf(preact * 0.7071067811865476))
    density = jnp.exp(-0.5 * preact * preact) * 0.3989422804014327
    return normal_cdf + preact * density


def local(activations, partner, mix_weight, weight, bias, earlier, cotangent):
    width = activations.shape[1]
    every_image = lax.all_gather(activations, "row", axis=0, tiled=True)
    image_count = every_image.shape[0] // PATCHES
    first_image = lax.axis_index("row") * IMG_DEV
    my_partner = lax.dynamic_slice_in_dim(partner, first_image, IMG_DEV)
    my_mix = lax.dynamic_slice_in_dim(mix_weight, first_image, IMG_DEV)
    other = every_image.reshape(image_count, PATCHES, width)[my_partner]
    share = (my_mix.astype(jnp.float32) / 256.0)[:, None, None]
    own_images = activations.reshape(IMG_DEV, PATCHES, width).astype(jnp.float32)
    blended = (share * own_images + (1.0 - share) * other.astype(jnp.float32)).astype(jnp.bfloat16)
    blended = blended.reshape(activations.shape[0], width)
    gathered = lax.all_gather(blended, "col", axis=1, tiled=True)
    product = jnp.dot(gathered, weight, preferred_element_type=jnp.float32)
    preact = earlier.astype(jnp.float32) + product + bias[None, :]
    normal_cdf = 0.5 * (1.0 + lax.erf(preact * 0.7071067811865476))
    hidden = (preact * normal_cdf).astype(jnp.bfloat16)
    grad_pre = (cotangent.astype(jnp.float32) * slope(preact)).astype(jnp.bfloat16)
    weight_grad = lax.psum_scatter(
        lax.dot_general(
            gathered, grad_pre, (((0,), (0,)), ((), ())), preferred_element_type=jnp.float32
        ).astype(jnp.bfloat16),
        "row",
        scatter_dimension=0,
        tiled=True,
    ).astype(jnp.float32)
    return (hidden, weight_grad)


def solution(mesh):
    return jax.shard_map(
        local,
        mesh=mesh,
        in_specs=(
            P("row", "col"),
            P(),
            P(),
            P(None, "col"),
            P("col"),
            P("row", "col"),
            P("row", "col"),
        ),
        out_specs=(P("row", "col"), P("row", "col")),
        check_vma=False,
    )
```

profile of v0, /device:TPU:8, one launch (start us, length us, event | category | flops | bytes accessed | tf_op | source)
XLA Modules:
  0.0 235.6 jit_solution(4898058432803832477)
XLA Ops:
  7.2 0.0 copy-start
  7.2 0.0 copy-start.1
  7.2 0.0 copy-start.2
  7.2 0.0 copy-start.5
  7.2 0.0 all-gather.2.cloned.1.call-start
  7.3 55.5 %all_gather.6 = bf16[16384,24]{0,1:T(8,128)(2,1)S(1)} all-gather(bf16[1024,24]{0,1:T(8,128)(2,1)} %param.7), channel_id=1, replica_groups=mesh['row'=16,'col'=32] {'row'}, dimensions={0}, use_global_device_ids=true | all-gather | bytes 835584 | tf_op jit(solution)/shard_map/all_gather | solution.py:18
  62.8 0.1 copy.16
  62.8 0.7 compare_select_fusion
  63.6 0.5 gather_fusion
  64.2 0.0 copy-done.2
  64.2 0.1 broadcast_subtract_fusion
  64.3 0.1 broadcast_bitcast_fusion
  64.3 0.0 copy-done.1
  64.3 0.6 add_convert_fusion
  65.0 0.0 all-gather.2.cloned.1.call-update
  65.0 0.0 copy-start.3
  65.0 0.0 reduce-scatter.2.cloned.1.call-start
  65.1 60.0 %all-gather.2.cloned.1.call-done = bf16[1024,768]{0,1:T(8,128)(2,1)} async-done(((bf16[1024,24]{0,1:T(8,128)(2,1)}), bf16[1024,768]{0,1:T(8,128)(2,1)}) %all-gather.2.cloned.1.call-update) | async-done | bytes 1572880 | tf_op jit(solution)/shard_map/all_gather | solution.py:28
  125.1 0.0 copy-done
  125.1 0.0 copy-done.5
  125.1 0.0 copy-start.4
  125.1 5.2 %multiply_convert_fusion = (bf16[1024,768]{1,0:T(8,128)(2,1)}, f32[1024,768]{1,0:T(8,128)S(1)}) fusion(f32[768]{0:T(1024)S(1)} %copy-done.5, bf16[1024,768]{0,1:T(8,128)(2,1)} %all-gather.2.cloned.1.call-done, bf16[768,768]{1,0:T(8,128)(2,1)S(1)} %copy-done, bf16[1024,768]{1,0:T(8,128)(2,1)} %param.12), kind=kOutput, calls=%fused_computation.8 | convolution fusion | flops 1214251008 | bytes 9047040 | tf_op jit(solution)/shard_map/dot_general | solution.py:29
  130.3 0.0 copy-done.3
  130.3 0.0 copy-done.4
  130.3 3.2 %fusion.10 = bf16[768,768]{1,0:T(8,128)(2,1)} fusion(bf16[1024,768]{0,1:T(8,128)(2,1)S(1)} %copy-done.4, f32[1024,768]{1,0:T(8,128)S(1)} %get-tuple-element.5, bf16[1024,768]{1,0:T(8,128)(2,1)S(1)} %copy-done.3), kind=kOutput, calls=%fused_computation.14 | convolution fusion | flops 1217200128 | bytes 7471104 | tf_op jit(solution)/shard_map/dot_general | solution.py:35
  133.5 0.0 reduce-scatter.2.cloned.1.call-update
  133.5 93.7 %reduce-scatter.2.cloned.1.call-done = bf16[48,768]{1,0:T(8,128)(2,1)} async-done(((bf16[768,768]{1,0:T(8,128)(2,1)}), bf16[48,768]{1,0:T(8,128)(2,1)}) %reduce-scatter.2.cloned.1.call-update) | async-done | bytes 73744 | tf_op jit(solution)/shard_map/reduce_scatter | solution.py:34
  227.2 1.6 convert_element_type.46
  (5 shorter events, 0.0 us)
Async XLA Ops:
  7.2 117.9 %copy-start = (bf16[768,768]{1,0:T(8,128)(2,1)S(1)}, bf16[768,768]{1,0:T(8,128)(2,1)}, u32[]{:S(2)}) copy-start(bf16[768,768]{1,0:T(8,128)(2,1)} %param.10) | copy-start | bytes 3538948
  7.2 57.2 %copy-start.1 = (bf16[1024,24]{0,1:T(8,128)(2,1)S(1)}, bf16[1024,24]{0,1:T(8,128)(2,1)}, u32[]{:S(2)}) copy-start(bf16[1024,24]{0,1:T(8,128)(2,1)} %param.7) | copy-start | bytes 147460
  7.2 57.0 %copy-start.2 = (s32[64]{0:T(128)S(1)}, s32[64]{0:T(128)}, u32[]{:S(2)}) copy-start(s32[64]{0:T(128)} %param.9) | copy-start | bytes 772
  7.2 117.9 %copy-start.5 = (f32[768]{0:T(1024)S(1)}, f32[768]{0:T(1024)}, u32[]{:S(2)}) copy-start(f32[768]{0:T(1024)} %param.11) | copy-start | bytes 9220
  7.2 117.9 %all-gather.2.cloned.1.call-start = ((), (), s32[]{:S(2)}) async-start(), calls=%async_computation.1 | async-start | bytes 1622016 | tf_op jit(solution)/shard_map/all_gather | solution.py:28
  65.0 65.3 %copy-start.3 = (bf16[1024,768]{1,0:T(8,128)(2,1)S(1)}, bf16[1024,768]{1,0:T(8,128)(2,1)}, u32[]{:S(2)}) copy-start(bf16[1024,768]{1,0:T(8,128)(2,1)} %param.13) | copy-start | bytes 4718596
  65.0 162.1 %reduce-scatter.2.cloned.1.call-start = ((), (), s32[]{:S(2)}) async-start(), calls=%async_computation.2 | async-start | bytes 1253376 | tf_op jit(solution)/shard_map/reduce_scatter | solution.py:34
  125.1 5.2 %copy-start.4 = (bf16[1024,768]{0,1:T(8,128)(2,1)S(1)}, bf16[1024,768]{0,1:T(8,128)(2,1)}, u32[]{:S(2)}) copy-start(bf16[1024,768]{0,1:T(8,128)(2,1)} %all-gather.2.cloned.1.call-done) | copy-start | bytes 4718596
Sparse Core Ops, SparseCore 0:
  65.1 59.8 all-gather.1
  133.6 93.5 reduce-scatter.1
where the time goes:
time: 236 us
  waiting for transfers between devices  154 us (65%)
  blocking collectives  55.5 us (24%)
  between operations  14.1 us (6%)
  matrix products  8.38 us (4%)
  other arithmetic  3.03 us (1%)
    reduce_scatter x1, waiting for transfers between devices, local(): lax.psum_scatter(lax.dot_general(gathered, grad_pre, (((0,), (0,)), ((),...  93.7 us
    all_gather x1, waiting for transfers between devices, local(): gathered = lax.all_gather(blended, 'col', axis=1, tiled=True)  60 us
    all_gather x1, blocking collectives, local(): every_image = lax.all_gather(activations, 'row', axis=0, tiled=True)  55.5 us
    dot_general x1, matrix products, local(): product = jnp.dot(gathered, weight, preferred_element_type=jnp.float32)  5.21 us
  transfers between devices with their start and end apart: 2, of which 2 were waited for; matrix products, arithmetic and copies ran while one was open for 0% of the time, Pallas kernels for 0%

commit v1 on v0

--- a/solution.py
+++ b/solution.py
@@ -25,7 +25,9 @@
     own_images = activations.reshape(IMG_DEV, PATCHES, width).astype(jnp.float32)
     blended = (share * own_images + (1.0 - share) * other.astype(jnp.float32)).astype(jnp.bfloat16)
     blended = blended.reshape(activations.shape[0], width)
-    gathered = lax.all_gather(blended, "col", axis=1, tiled=True)
+    gathered = jnp.concatenate(
+        lax.all_to_all(jnp.stack([blended] * lax.axis_size("col")), "col", 0, 0), axis=1
+    )
     product = jnp.dot(gathered, weight, preferred_element_type=jnp.float32)
     preact = earlier.astype(jnp.float32) + product + bias[None, :]
     normal_cdf = 0.5 * (1.0 + lax.erf(preact * 0.7071067811865476))

time: 236 us -> 210 us (0.89)
  waiting for transfers between devices: 154 us -> 82.6 us
  blocking collectives: 55.5 us -> 103 us
    all_gather x1 -> x0, waiting for transfers between devices: 60 us -> none  [local(): gathered = lax.all_gather(blended, 'col', axis=1, tiled=True)]
    all_to_all x0 -> x1, blocking collectives: none -> 47.9 us  [local(): lax.all_to_all(jnp.stack([blended] * lax.axis_size('col')), 'col', 0, 0)]
    reduce_scatter x1, waiting for transfers between devices: 93.7 us -> 82.6 us  [local(): lax.psum_scatter(lax.dot_general(gathered, grad_pre, (((0,), (0,)), ((),...]
  transfers between devices with their start and end apart: 2 -> 1, of which waited for: 2 -> 1; matrix products, arithmetic and copies ran while one was open for 0% -> 0% of each run, Pallas kernels for 0% -> 0%
where the time goes in v1:
time: 210 us
  blocking collectives  103 us (49%)
  waiting for transfers between devices  82.6 us (39%)
  between operations  14.1 us (7%)
  matrix products  6.63 us (3%)
  other arithmetic  2.41 us (1%)
    reduce_scatter x1, waiting for transfers between devices, local(): lax.psum_scatter(lax.dot_general(gathered, grad_pre, (((0,), (0,)), ((),...  82.6 us
    all_gather x1, blocking collectives, local(): every_image = lax.all_gather(activations, 'row', axis=0, tiled=True)  55.5 us
    all_to_all x1, blocking collectives, local(): lax.all_to_all(jnp.stack([blended] * lax.axis_size('col')), 'col', 0, 0)  47.9 us
  transfers between devices with their start and end apart: 1, of which 1 were waited for; matrix products, arithmetic and copies ran while one was open for 0% of the time, Pallas kernels for 0%

profile of v1, /device:TPU:8, one launch (start us, length us, event | category | flops | bytes accessed | tf_op | source)
XLA Modules:
  0.0 210.1 jit_solution(17366559537369503979)
XLA Ops:
  7.2 0.0 copy-start
  7.2 0.0 copy-start.1
  7.2 0.0 copy-start.2
  7.2 0.0 reduce-scatter.2.cloned.1.call-start
  7.2 55.5 %all_gather.3 = bf16[16384,24]{0,1:T(8,128)(2,1)S(1)} all-gather(bf16[1024,24]{0,1:T(8,128)(2,1)} %param.7), channel_id=1, replica_groups=mesh['row'=16,'col'=32] {'row'}, dimensions={0}, use_global_device_ids=true | all-gather | bytes 835584 | tf_op jit(solution)/shard_map/all_gather | solution.py:18
  62.8 0.1 copy.17
  62.8 0.0 copy-start.5
  62.8 0.7 compare_select_fusion
  63.6 0.5 gather_fusion
  64.1 0.0 copy-start.3
  64.2 0.0 copy-done.2
  64.2 0.1 broadcast_subtract_fusion
  64.3 0.1 broadcast_bitcast_fusion
  64.3 0.0 copy-done.1
  64.4 0.2 stack.3
  64.6 47.9 %all_to_all.5 = bf16[32,1024,24]{1,2,0:T(8,128)(2,1)S(1)} all-to-all(bf16[32,1024,24]{1,2,0:T(8,128)(2,1)S(1)} %stack.3), channel_id=1, replica_groups=mesh['row'=16,'col'=32] {'col'}, dimensions={0} | all-to-all | bytes 3145728 | tf_op jit(solution)/shard_map/all_to_all | solution.py:29
  112.4 0.0 copy-done
  112.4 0.0 copy-done.5
  112.4 0.0 copy-done.3
  112.4 0.0 copy-start.4
  112.5 3.5 %multiply_convert_fusion = (bf16[1024,768]{1,0:T(8,128)(2,1)}, f32[1024,768]{1,0:T(8,128)S(1)}) fusion(f32[768]{0:T(1024)S(1)} %copy-done.5, bf16[1024,768]{0,1:T(8,128)(2,1)S(1)} %bitcast.20, bf16[768,768]{1,0:T(8,128)(2,1)S(1)} %copy-done, bf16[1024,768]{1,0:T(8,128)(2,1)S(1)} %copy-done.3), kind=kOutput, calls=%fused_computation.8 | convolution fusion | flops 1214251008 | bytes 9047040 | tf_op jit(solution)/shard_map/dot_general | solution.py:31
  115.9 0.0 copy-done.4
  115.9 3.2 %fusion.10 = bf16[768,768]{1,0:T(8,128)(2,1)} fusion(bf16[1024,768]{0,1:T(8,128)(2,1)S(1)} %bitcast.21, f32[1024,768]{1,0:T(8,128)S(1)} %get-tuple-element.5, bf16[1024,768]{1,0:T(8,128)(2,1)S(1)} %copy-done.4), kind=kOutput, calls=%fused_computation.14 | convolution fusion | flops 1217200128 | bytes 7471104 | tf_op jit(solution)/shard_map/dot_general | solution.py:37
  119.1 0.0 reduce-scatter.2.cloned.1.call-update
  119.1 82.6 %reduce-scatter.2.cloned.1.call-done = bf16[48,768]{1,0:T(8,128)(2,1)} async-done(((bf16[768,768]{1,0:T(8,128)(2,1)}), bf16[48,768]{1,0:T(8,128)(2,1)}) %reduce-scatter.2.cloned.1.call-update) | async-done | bytes 73744 | tf_op jit(solution)/shard_map/reduce_scatter | solution.py:36
  201.7 1.6 convert_element_type.49
  (6 shorter events, 0.1 us)
Async XLA Ops:
  7.2 105.3 %copy-start = (bf16[768,768]{1,0:T(8,128)(2,1)S(1)}, bf16[768,768]{1,0:T(8,128)(2,1)}, u32[]{:S(2)}) copy-start(bf16[768,768]{1,0:T(8,128)(2,1)} %param.10) | copy-start | bytes 3538948
  7.2 57.2 %copy-start.1 = (bf16[1024,24]{0,1:T(8,128)(2,1)S(1)}, bf16[1024,24]{0,1:T(8,128)(2,1)}, u32[]{:S(2)}) copy-start(bf16[1024,24]{0,1:T(8,128)(2,1)} %param.7) | copy-start | bytes 147460
  7.2 57.0 %copy-start.2 = (s32[64]{0:T(128)S(1)}, s32[64]{0:T(128)}, u32[]{:S(2)}) copy-start(s32[64]{0:T(128)} %param.9) | copy-start | bytes 772
  7.2 194.5 %reduce-scatter.2.cloned.1.call-start = ((), (), s32[]{:S(2)}) async-start(), calls=%async_computation.2 | async-start | bytes 1253376 | tf_op jit(solution)/shard_map/reduce_scatter | solution.py:36
  62.8 49.6 %copy-start.5 = (f32[768]{0:T(1024)S(1)}, f32[768]{0:T(1024)}, u32[]{:S(2)}) copy-start(f32[768]{0:T(1024)} %param.11) | copy-start | bytes 9220
  64.1 48.3 %copy-start.3 = (bf16[1024,768]{1,0:T(8,128)(2,1)S(1)}, bf16[1024,768]{1,0:T(8,128)(2,1)}, u32[]{:S(2)}) copy-start(bf16[1024,768]{1,0:T(8,128)(2,1)} %param.12) | copy-start | bytes 4718596
  112.4 3.5 %copy-start.4 = (bf16[1024,768]{1,0:T(8,128)(2,1)S(1)}, bf16[1024,768]{1,0:T(8,128)(2,1)}, u32[]{:S(2)}) copy-start(bf16[1024,768]{1,0:T(8,128)(2,1)} %param.13) | copy-start | bytes 4718596
Sparse Core Ops, SparseCore 0:
  119.2 82.4 reduce-scatter.1
